TPU v7x, 32 devices: a whole 2x2x4 slice. The times are simulated.
32 devices in a mesh: pipe: 4 (over y, core), expert: 4 (over z), dp: 2 (over x).
Axes of the slice: x: 2, y: 2, z: 4, core: 2. Of those that a mesh axis runs over, the one named last changes fastest.
Arguments:
- section_grad: bfloat16 [4, 1024, 7168], P('pipe', ('expert', 'dp')), may hold values from -6 to 6
- loss_grad: bfloat16 [1024, 7168], P(('expert', 'dp')), may hold values from -6 to 6
- expert_ids: int32 [4, 1024, 8], P('pipe', ('expert', 'dp')), may hold values from 0 to 255, all different within a row
- gate_values: bfloat16 [4, 1024, 8], P('pipe', ('expert', 'dp')), may hold values from 0.049804688 to 0.59765625
- down_inputs: bfloat16 [4, 2, 16, 1024], P('pipe', 'dp', None, 'expert'), may hold values from -1.59375 to 1.59375
Outputs:
- down_grad: bfloat16 [4, 7168, 1024], P('pipe', 'dp', 'expert')
Inputs may be any that keep to these rules, and one draw needn't show every extreme that they name: `expert_ids`: each row names 8 different experts; every expert is named by some row.
All inputs are finite; a program needn't handle non-finite values.
Results may differ from a plain program's by a relative error of at most 0.009.
Values may be sent and summed in bfloat16 or wider, within the bound.
A program may use at most 64 MiB of HBM per device.

v0:
```python
import jax
import jax.numpy as jnp
from jax import lax
from jax.sharding import PartitionSpec as P

ROUTED = 256
TOPK = 8
SPLIT = 4


def from_behind(value, axis, steps):
    count = lax.axis_size(axis)
    leading, last = (max(0, -steps), min(count, count - steps))
    return lax.ppermute(value, axis, [(source, source + steps) for source in range(leading, last)])


def compact_rows(id_block, gate_block, grad_rows, experts, capacity):
    flat_ids = id_block.reshape(-1)
    onehot = (flat_ids[:, None] == jnp.arange(experts, dtype=jnp.int32)[None, :]).astype(jnp.int32)
    before = jnp.cumsum(onehot, axis=0) - onehot
    ranks = jnp.sum(before * onehot, axis=1)
    retained = (flat_ids < experts) & (ranks < capacity)
    target = jnp.where(retained, flat_ids * capacity + ranks, -1).reshape(id_block.shape)
    wanted = jnp.arange(experts * capacity, dtype=jnp.int32)
    matches = target[None, :, :] == wanted[:, None, None]
    selector = jnp.sum(
        jnp.where(matches, gate_block[None, :, :].astype(jnp.float32), 0.0), axis=2
    ).astype(jnp.bfloat16)
    return jnp.dot(selector, grad_rows, preferred_element_type=jnp.float32).astype(jnp.bfloat16)


def local(section_grad, loss_grad, expert_ids, gate_values, down_inputs):
    expert_count = lax.axis_size("expert")
    group_count = lax.axis_size("dp")
    experts = expert_count // SPLIT
    tokens_dev = section_grad.shape[1]
    model_width = section_grad.shape[2]
    capacity = tokens_dev * TOPK // ROUTED
    last_section = lax.axis_index("pipe") == lax.axis_size("pipe") - 1
    received = from_behind(section_grad[0], "pipe", -1)
    upstream = jnp.where(last_section, loss_grad, received)
    compact = compact_rows(expert_ids[0], gate_values[0], upstream, experts, capacity)
    spread_rows = jnp.broadcast_to(
        compact.reshape(experts, 1, capacity, model_width), (experts, SPLIT, capacity, model_width)
    )
    outgoing = spread_rows.reshape(expert_count, capacity, model_width)
    arrived = lax.all_to_all(outgoing, "expert", split_axis=0, concat_axis=0, tiled=True)
    slot_rows = arrived.reshape(expert_count * capacity, model_width)
    saved_inputs = down_inputs[0, 0]
    spread = jnp.tile(saved_inputs, (1, group_count))
    own_part, all_inputs = (
        lax.all_to_all(slot_rows, "dp", split_axis=1, concat_axis=0, tiled=True),
        lax.all_to_all(spread, "dp", split_axis=1, concat_axis=0, tiled=True),
    )
    own_part = own_part.reshape(group_count, expert_count * capacity, model_width // group_count)
    all_inputs = all_inputs.reshape(group_count, expert_count * capacity, saved_inputs.shape[1])
    partials = jnp.einsum("gsd,gsh->gdh", own_part, all_inputs, preferred_element_type=jnp.float32)
    rounded = lax.optimization_barrier(partials.astype(jnp.bfloat16))
    summed = jnp.sum(rounded.astype(jnp.float32), axis=0)
    return summed.astype(jnp.bfloat16)[None]


def solution(mesh):
    in_specs = (
        P("pipe", ("expert", "dp"), None),
        P(("expert", "dp"), None),
        P("pipe", ("expert", "dp"), None),
        P("pipe", ("expert", "dp"), None),
        P("pipe", "dp", None, "expert"),
    )
    out_specs = P("pipe", "dp", "expert")
    return jax.shard_map(local, mesh=mesh, in_specs=in_specs, out_specs=out_specs, check_vma=False)
```

profile of v0, /device:TPU:4, one launch (start us, length us, event | category | flops | bytes accessed | tf_op | source)
XLA Modules:
  0.0 57.5 jit_solution(10418955877688960487)
XLA Ops:
  0.0 1.9 %collective-permute-start = (bf16[128,7168]{1,0:T(8,128)(2,1)}, bf16[128,7168]{1,0:T(8,128)(2,1)S(1)}, u32[]{:S(2)}, u32[]{:S(2)}) collective-permute-start(bf16[128,7168]{1,0:T(8,128)(2,1)} %bitcast.22), channel_id=1, source_target_pairs={{8,0},{16,8},{24,16},{9,1},{17,9},{25,17},{10,2},{18,10},{26,18},{... | collective-permute-start | bytes 5505032 | tf_op jit(solution)/shard_map/ppermute | solution.py:14
  1.9 0.7 %fusion.4 = s32[1,128,8]{1,2,0:T(8,128)S(1)} fusion(s32[1,128,8]{1,2,0:T(8,128)} %param.7), kind=kLoop, calls=%fused_computation.13 | loop fusion | flops 2048 | bytes 8192 | tf_op jit(solution)/shard_map/convert_element_type | solution.py:19
  2.6 0.1 copy.27
  2.7 0.1 reshape.109
  2.8 0.3 reduce-window.6
  3.1 0.1 reshape.104
  3.2 0.2 slice_reduce_fusion
  3.4 0.2 reduce-window.9
  3.6 0.1 broadcast.41
  3.6 0.1 reshape.107
  3.8 0.1 copy.28
  3.8 0.7 %bitcast_convert_fusion = f32[128,8]{0,1:T(8,128)S(1)} fusion(bf16[1,128,8]{1,2,0:T(8,128)(2,1)} %param.8), kind=kLoop, calls=%fused_computation.11 | loop fusion | flops 1024 | bytes 6144 | tf_op jit(solution)/shard_map/jit(_where)/broadcast_in_dim | solution.py:27
  4.5 0.7 %select_bitcast_fusion = s32[128,8]{0,1:T(8,128)S(1)} fusion(s32[1,128,8]{1,2,0:T(8,128)} %param.7, s32[1,128,8]{1,2,0:T(8,128)S(1)} %copy.28, s32[1,128,8]{1,2,0:T(8,128)S(1)} %copy.29), kind=kLoop, calls=%fused_computation.8 | loop fusion | flops 11264 | bytes 16384 | tf_op jit(solution)/shard_map/eq | solution.py:25
  5.3 0.0 copy-start
  5.3 17.7 %collective-permute-done = bf16[128,7168]{1,0:T(8,128)(2,1)S(1)} collective-permute-done((bf16[128,7168]{1,0:T(8,128)(2,1)}, bf16[128,7168]{1,0:T(8,128)(2,1)S(1)}, u32[]{:S(2)}, u32[]{:S(2)}) %collective-permute-start) | collective-permute-done | bytes 1835040 | tf_op jit(solution)/shard_map/ppermute | solution.py:14
  23.0 0.4 convolution_convert_fusion
  23.4 0.1 reshape.108
  23.5 11.6 %all_to_all.34 = bf16[4,4,7168]{2,1,0:T(4,128)(2,1)S(1)} all-to-all(bf16[4,4,7168]{2,1,0:T(4,128)(2,1)S(1)} %reshape.108), channel_id=1, replica_groups=mesh['pipe'=4,'expert'=4,'dp'=2] {'expert'}, dimensions={0} | all-to-all | bytes 458752 | tf_op jit(solution)/shard_map/all_to_all | solution.py:47
  35.0 0.0 copy-done
  35.0 0.6 %tile.9 = bf16[16,2,256]{2,0,1:T(8,128)(2,1)} broadcast(bf16[16,256]{1,0:T(8,128)(2,1)S(1)} %bitcast.20), dimensions={0,2} | broadcast | bytes 24576 | tf_op jit(solution)/shard_map/tile | solution.py:50
  35.6 3.2 %all-to-all-start.2 = ((bf16[16,2,256]{2,0,1:T(8,128)(2,1)}), bf16[16,2,256]{2,0,1:T(8,128)(2,1)S(1)}, u32[]{:S(2)}, u32[]{:S(2)}) async-start(bf16[16,2,256]{2,0,1:T(8,128)(2,1)} %tile.9), calls=%async_computation.2 | async-start | bytes 32768 | tf_op jit(solution)/shard_map/all_to_all | solution.py:53
  38.9 0.1 all_to_all.26
  39.0 3.7 %all-to-all-done.2 = bf16[16,2,256]{2,0,1:T(8,128)(2,1)S(1)} async-done(((bf16[16,2,256]{2,0,1:T(8,128)(2,1)}), bf16[16,2,256]{2,0,1:T(8,128)(2,1)S(1)}, u32[]{:S(2)}, u32[]{:S(2)}) %all-to-all-start.2) | async-done | bytes 16416 | tf_op jit(solution)/shard_map/all_to_all | solution.py:53
  42.7 7.4 %all_to_all.35 = bf16[16,2,3584]{2,0,1:T(8,128)(2,1)S(1)} all-to-all(bf16[16,2,3584]{2,0,1:T(8,128)(2,1)S(1)} %copy.30), channel_id=1, replica_groups=mesh['pipe'=4,'expert'=4,'dp'=2] {'dp'}, dimensions={1} | all-to-all | bytes 458752 | tf_op jit(solution)/shard_map/all_to_all | solution.py:52
  50.1 3.0 %convolution_convert_fusion.1 = bf16[2,3584,256]{2,1,0:T(8,128)(2,1)} fusion(bf16[16,2,3584]{2,0,1:T(8,128)(2,1)S(1)} %all_to_all.35, bf16[16,2,256]{2,0,1:T(8,128)(2,1)S(1)} %all-to-all-done.2), kind=kOutput, calls=%fused_computation.1 | convolution fusion | flops 60555264 | bytes 3915776 | tf_op jit(solution)/shard_map/gsd,gsh->gdh/dot_general | solution.py:57
  53.0 4.5 %reduce_sum.26 = bf16[3584,256]{1,0:T(8,128)(2,1)} reduce(bf16[2,3584,256]{2,1,0:T(8,128)(2,1)} %convolution_convert_fusion.1, bf16[]{:T(256)} %constant.23.clone.1), dimensions={0}, to_apply=%region_3.4 | reduce | flops 917504 | bytes 5505026 | tf_op jit(solution)/shard_map/reduce_sum | solution.py:59
  (4 shorter events, 0.1 us)
Async XLA Ops:
  0.0 23.0 %collective-permute-start = (bf16[128,7168]{1,0:T(8,128)(2,1)}, bf16[128,7168]{1,0:T(8,128)(2,1)S(1)}, u32[]{:S(2)}, u32[]{:S(2)}) collective-permute-start(bf16[128,7168]{1,0:T(8,128)(2,1)} %bitcast.22), channel_id=1, source_target_pairs={{8,0},{16,8},{24,16},{9,1},{17,9},{25,17},{10,2},{18,10},{26,18},{... | collective-permute-start | bytes 5505032 | tf_op jit(solution)/shard_map/ppermute | solution.py:14
  5.3 29.8 %copy-start = (bf16[1,1,16,256]{3,2,1,0:T(8,128)(2,1)S(1)}, bf16[1,1,16,256]{3,2,1,0:T(8,128)(2,1)}, u32[]{:S(2)}) copy-start(bf16[1,1,16,256]{3,2,1,0:T(8,128)(2,1)} %param.9) | copy-start | bytes 24580
  35.6 7.1 %all-to-all-start.2 = ((bf16[16,2,256]{2,0,1:T(8,128)(2,1)}), bf16[16,2,256]{2,0,1:T(8,128)(2,1)S(1)}, u32[]{:S(2)}, u32[]{:S(2)}) async-start(bf16[16,2,256]{2,0,1:T(8,128)(2,1)} %tile.9), calls=%async_computation.2 | async-start | bytes 32768 | tf_op jit(solution)/shard_map/all_to_all | solution.py:53
where the time goes:
time: 57.9 us; the launch traced here: 57.5 us
  waiting for transfers between devices  21.4 us (37%)
  blocking collectives  18.9 us (33%)
  other arithmetic  7.06 us (12%)
  starting transfers between devices  5.14 us (9%)
  matrix products  3.39 us (6%)
  local copies, waits for them, and re-layouts  1.53 us (3%)
    ppermute x1, waiting for transfers between devices, from_behind(): lax.ppermute(value, axis, [(source, source + steps) for source in range(l...  17.7 us
    all_to_all x1, blocking collectives, local(): lax.all_to_all(outgoing, 'expert', split_axis=0, concat_axis=0, tiled=True)  11.6 us
    all_to_all x1, blocking collectives, local(): lax.all_to_all(slot_rows, 'dp', split_axis=1, concat_axis=0, tiled=True)  7.35 us
    reduce_sum x1, other arithmetic, local(): summed = jnp.sum(rounded.astype(jnp.float32), axis=0)  4.48 us
    all_to_all x1, waiting for transfers between devices, local(): lax.all_to_all(spread, 'dp', split_axis=1, concat_axis=0, tiled=True)  3.71 us
    all_to_all x1, starting transfers between devices, local(): lax.all_to_all(spread, 'dp', split_axis=1, concat_axis=0, tiled=True)  3.24 us
    dot_general x1, matrix products, local(): jnp.einsum('gsd,gsh->gdh', own_part, all_inputs, preferred_element_type=j...  2.95 us
    ppermute x1, starting transfers between devices, from_behind(): lax.ppermute(value, axis, [(source, source + steps) for source in range(l...  1.91 us
  transfers between devices with their start and end apart: 2, of which 2 were waited for; matrix products, arithmetic and copies ran while one was open for 6% of the time, Pallas kernels for 0%

commit v1 on v0

v1 whole, which is shorter than its diff:
```python
import functools

import jax
import jax.numpy as jnp
from jax import lax
from jax.experimental import pallas as pl
from jax.experimental.pallas import tpu as pltpu
from jax.sharding import PartitionSpec as P

ROUTED = 256
SPLIT = 4
TILE = 16
LANES = 128
VMEM = pl.BlockSpec(memory_space=pltpu.VMEM)
ANY = pl.BlockSpec(memory_space=pl.ANY)


def each(count, body):
    if count <= 16:
        for i in range(count):
            body(i)
    else:
        lax.fori_loop(0, count, lambda i, c: (body(i), c)[1], 0)


def dot(a, b, contract):
    return lax.dot_general(a, b, ((contract[0], contract[1]), ((), ())), preferred_element_type=jnp.float32)


def chunk_starts(width, pack):
    size = -(-width // (pack * LANES)) * LANES
    return size, [min(c * size, width - size) for c in range(pack)]


def make_selector(ids, gates, expert, cap):
    tokens = ids.shape[1]
    found = ids == expert
    ones = jnp.ones((TILE, ids.shape[0]), jnp.float32)
    hit = jnp.sum(jnp.where(found, 1.0, 0.0), axis=0, keepdims=True)
    gate = jnp.sum(jnp.where(found, gates, 0.0), axis=0, keepdims=True)
    hit = jnp.broadcast_to(hit, (TILE, tokens))
    gate = jnp.broadcast_to(gate, (TILE, tokens))
    earlier = lax.broadcasted_iota(jnp.int32, (tokens, tokens), 0) < lax.broadcasted_iota(
        jnp.int32, (tokens, tokens), 1
    )
    before = jnp.where(earlier, 1.0, 0.0).astype(jnp.bfloat16)
    rank = dot(hit.astype(jnp.bfloat16), before, ((1,), (0,)))
    row = lax.broadcasted_iota(jnp.int32, (TILE, tokens), 0) % cap
    keep = (hit > 0.5) & (rank.astype(jnp.int32) == row)
    return jnp.where(keep, gate, 0.0).astype(jnp.bfloat16)


def gather_kernel(
    cap, ids_ref, gate_ref, grad_hbm, loss_hbm, inputs_ref,
    rows_ref, all_inputs_ref,
    sel_own, sel_in, grad_v, loss_v, out_a, out_b,
    load_sem, sel_sem, in_send, in_recv, send_a, send_b, recv_sem,
):
    pipes, cols, groups = lax.axis_size("pipe"), lax.axis_size("expert"), lax.axis_size("dp")
    p, e, g = lax.axis_index("pipe"), lax.axis_index("expert"), lax.axis_index("dp")
    experts = cols // SPLIT
    pack = TILE // cap
    width = grad_v.shape[1] // groups
    slots = inputs_ref.shape[0]
    size, starts = chunk_starts(width, pack)
    count = cols * groups
    me = e * groups + g
    last = p == pipes - 1
    slot = g * cols + e

    def place(pipe, col, group):
        return {"pipe": pipe, "expert": col, "dp": group}

    def load(src, dst, base, h):
        span = pl.ds(h * width, width)
        return pltpu.make_async_copy(src.at[:, span], dst.at[:, span], load_sem.at[base + h])

    def row_copy(pipe, i, source, sems):
        col, group = i // groups, i % groups
        return pltpu.make_async_remote_copy(
            src_ref=source.at[(col // SPLIT) * groups + group],
            dst_ref=rows_ref.at[slot],
            send_sem=sems.at[i],
            recv_sem=recv_sem.at[slot],
            device_id=place(pipe, col, group),
            device_id_type=pl.DeviceIdType.MESH,
        )

    def selector_copy():
        return pltpu.make_async_remote_copy(
            src_ref=sel_own, dst_ref=sel_in, send_sem=sel_sem.at[0], recv_sem=sel_sem.at[1],
            device_id=place(lax.rem(p + 1, pipes), e, g), device_id_type=pl.DeviceIdType.MESH,
        )

    def inputs_copy(group):
        return pltpu.make_async_remote_copy(
            src_ref=inputs_ref, dst_ref=all_inputs_ref.at[g],
            send_sem=in_send.at[group], recv_sem=in_recv.at[g],
            device_id=place(p, e, group), device_id_type=pl.DeviceIdType.MESH,
        )

    def other_group(k):
        return lax.rem(g + 1 + k, groups)

    def other_device(k):
        return lax.rem(me + 1 + k, count)

    @pl.when(last)
    def _():
        for h in range(groups):
            load(loss_hbm, loss_v, groups, h).start()

    @pl.when(p >= 1)
    def _():
        for h in range(groups):
            load(grad_hbm, grad_v, 0, h).start()

    barrier = pltpu.get_barrier_semaphore()

    def greet(pipe, col, group):
        pl.semaphore_signal(
            barrier, inc=1, device_id=place(pipe, col, group), device_id_type=pl.DeviceIdType.MESH
        )

    @pl.when(p >= 1)
    def _():
        greet(p - 1, e, g)

    for k in range(groups - 1):
        greet(p, e, other_group(k))

    @pl.when(jnp.logical_not(last))
    def _():
        each(count, lambda i: greet(p + 1, i // groups, i % groups))

    @pl.when(last)
    def _():
        def one(k):
            i = other_device(k)
            greet(p, i // groups, i % groups)
        each(count - 1, one)

    ids = ids_ref[...]
    gates = gate_ref[...].astype(jnp.float32)
    for x in range(experts):
        sel_own[x] = make_selector(ids, gates, x, cap)
    all_inputs_ref[g] = inputs_ref[...]

    targets = groups - 1 + jnp.where(p >= 1, count, 0) + jnp.where(last, count - 1, 1)
    pl.semaphore_wait(barrier, targets)

    @pl.when(jnp.logical_not(last))
    def _():
        selector_copy().start()

    for k in range(groups - 1):
        inputs_copy(other_group(k)).start()

    def pick(sel_ref, values, out, h):
        for x in range(experts):
            sel = sel_ref[x].astype(jnp.float32)
            chunk = lax.broadcasted_iota(jnp.int32, sel.shape, 0) // cap
            total = None
            for c in range(pack):
                part = jnp.where(chunk == c, sel, 0.0).astype(jnp.bfloat16)
                term = dot(part, values[:, pl.ds(h * width + starts[c], size)], ((1,), (0,)))
                total = term if total is None else total + term
            out[x * groups + h] = total.astype(jnp.bfloat16)

    @pl.when(last)
    def _():
        for h in range(groups):
            load(loss_hbm, loss_v, groups, h).wait()
            pick(sel_own, loss_v, out_b, h)
        rows_ref[slot] = out_b[(e // SPLIT) * groups + g]
        each(count - 1, lambda k: row_copy(p, other_device(k), out_b, send_b).start())

    @pl.when(p >= 1)
    def _():
        selector_copy().wait_recv()
        for h in range(groups):
            load(grad_hbm, grad_v, 0, h).wait()
            pick(sel_in, grad_v, out_a, h)
            each(cols, lambda k: row_copy(p - 1, k * groups + h, out_a, send_a).start())

    def arrived(i):
        return pltpu.make_async_remote_copy(
            src_ref=out_a.at[0], dst_ref=rows_ref.at[i], send_sem=send_a.at[0], recv_sem=recv_sem.at[i],
            device_id=place(p, e, g), device_id_type=pl.DeviceIdType.MESH,
        )

    @pl.when(jnp.logical_not(last))
    def _():
        each(count, lambda i: arrived(i).wait_recv())
        selector_copy().wait_send()

    @pl.when(last)
    def _():
        each(count - 1, lambda k: arrived(lax.rem(slot + 1 + k, count)).wait_recv())
        each(count - 1, lambda k: row_copy(p, other_device(k), out_b, send_b).wait_send())

    @pl.when(p >= 1)
    def _():
        each(count, lambda i: row_copy(p - 1, i, out_a, send_a).wait_send())

    for k in range(groups - 1):
        group = other_group(k)
        pltpu.make_async_remote_copy(
            src_ref=inputs_ref, dst_ref=all_inputs_ref.at[group],
            send_sem=in_send.at[group], recv_sem=in_recv.at[group],
            device_id=place(p, e, group), device_id_type=pl.DeviceIdType.MESH,
        ).wait()


def product_kernel(cap, starts, rows_ref, inputs_ref, out_ref):
    sources, tile, size = rows_ref.shape
    pack = tile // cap
    depth = sources * tile
    groups, slots, hidden = inputs_ref.shape
    inputs = inputs_ref[...].reshape(groups * slots, hidden)
    r = lax.broadcasted_iota(jnp.int32, (depth, groups * slots), 0)
    s = lax.broadcasted_iota(jnp.int32, (depth, groups * slots), 1)
    spread = jnp.where((r // tile == s // cap) & (r % cap == s % cap), 1.0, 0.0).astype(jnp.bfloat16)
    wide = dot(spread, inputs, ((1,), (0,)))
    chunk = (lax.broadcasted_iota(jnp.int32, wide.shape, 0) // cap) % pack
    weights = jnp.concatenate(
        [jnp.where(chunk == c, wide, 0.0).astype(jnp.bfloat16) for c in range(pack)], axis=1
    )
    for k in range(size // LANES):
        part = rows_ref[:, :, k * LANES:(k + 1) * LANES].reshape(depth, LANES)
        value = dot(part, weights, ((0,), (0,))).astype(out_ref.dtype)
        for c in range(pack):
            out_ref[starts[c] + k * LANES:starts[c] + (k + 1) * LANES, :] = value[:, c * hidden:(c + 1) * hidden]


def local(section_grad, loss_grad, expert_ids, gate_values, down_inputs):
    cols, groups = lax.axis_size("expert"), lax.axis_size("dp")
    experts = cols // SPLIT
    tokens, depth = section_grad.shape[1:]
    topk = expert_ids.shape[2]
    cap = tokens * topk // ROUTED
    pack = TILE // cap
    width = depth // groups
    size, starts = chunk_starts(width, pack)
    slots, hidden = down_inputs.shape[2:]
    count = cols * groups
    bf16 = jnp.bfloat16
    dma = pltpu.SemaphoreType.DMA
    rows, inputs = pl.pallas_call(
        functools.partial(gather_kernel, cap),
        out_shape=[
            jax.ShapeDtypeStruct((count, TILE, size), bf16),
            jax.ShapeDtypeStruct((groups, slots, hidden), bf16),
        ],
        in_specs=[VMEM, VMEM, ANY, ANY, VMEM],
        out_specs=[VMEM, VMEM],
        scratch_shapes=[
            pltpu.VMEM((experts, TILE, tokens), bf16),
            pltpu.VMEM((experts, TILE, tokens), bf16),
            pltpu.VMEM((tokens, depth), bf16),
            pltpu.VMEM((tokens, depth), bf16),
            pltpu.VMEM((experts * groups, TILE, size), bf16),
            pltpu.VMEM((experts * groups, TILE, size), bf16),
            dma((2 * groups,)),
            dma((2,)),
            dma((groups,)),
            dma((groups,)),
            dma((count,)),
            dma((count,)),
            dma((count,)),
        ],
        compiler_params=pltpu.CompilerParams(
            collective_id=0, has_side_effects=True, vmem_limit_bytes=32 << 20
        ),
    )(
        jnp.swapaxes(expert_ids[0], 0, 1),
        jnp.swapaxes(gate_values[0], 0, 1),
        section_grad[0],
        loss_grad,
        down_inputs[0, 0],
    )
    out = pl.pallas_call(
        functools.partial(product_kernel, cap, starts),
        out_shape=jax.ShapeDtypeStruct((width, hidden), bf16),
        in_specs=[VMEM, VMEM],
        out_specs=VMEM,
        compiler_params=pltpu.CompilerParams(vmem_limit_bytes=32 << 20),
    )(rows, inputs)
    return out[None]


def solution(mesh):
    in_specs = (
        P("pipe", ("expert", "dp"), None),
        P(("expert", "dp"), None),
        P("pipe", ("expert", "dp"), None),
        P("pipe", ("expert", "dp"), None),
        P("pipe", "dp", None, "expert"),
    )
    out_specs = P("pipe", "dp", "expert")
    return jax.shard_map(local, mesh=mesh, in_specs=in_specs, out_specs=out_specs, check_vma=False)
```

time: 57.9 us -> 21.5 us (0.37)
  the two profiles are of different devices: /device:TPU:4 before, /device:TPU:6 now
where the time goes in v1:
time: 21.5 us; the launch traced here: 21.2 us
  Pallas kernels  16.2 us (75%)
  local copies, waits for them, and re-layouts  5.06 us (24%)
    pallas_call x1, Pallas kernels, local(): pl.pallas_call(functools.partial(gather_kernel, cap), out_shape=[jax.Shap...  14.2 us
    unnamed x10, local copies, waits for them, and re-layouts  5.06 us
    pallas_call x1, Pallas kernels, local(): pl.pallas_call(functools.partial(product_kernel, cap, starts), out_shape=...  2 us

profile of v1, /device:TPU:6, one launch (start us, length us, event | category | flops | bytes accessed | tf_op | source)
XLA Modules:
  0.0 21.2 jit_solution(13532571530267164868)
XLA Ops:
  0.0 0.0 copy-start
  0.0 1.5 %copy-done = bf16[1,128,7168]{2,1,0:T(8,128)(2,1)S(1)} copy-done((bf16[1,128,7168]{2,1,0:T(8,128)(2,1)S(1)}, bf16[1,128,7168]{2,1,0:T(8,128)(2,1)}, u32[]{:S(2)}) %copy-start) | copy-done | bytes 1835032
  1.5 0.0 copy-start.1
  1.5 1.5 %copy-done.1 = bf16[128,7168]{1,0:T(8,128)(2,1)S(1)} copy-done((bf16[128,7168]{1,0:T(8,128)(2,1)S(1)}, bf16[128,7168]{1,0:T(8,128)(2,1)}, u32[]{:S(2)}) %copy-start.1) | copy-done | bytes 1835032
  3.0 0.0 copy-start.2
  3.0 0.7 %copy-done.2 = bf16[1,1,16,256]{3,2,1,0:T(8,128)(2,1)S(1)} copy-done((bf16[1,1,16,256]{3,2,1,0:T(8,128)(2,1)S(1)}, bf16[1,1,16,256]{3,2,1,0:T(8,128)(2,1)}, u32[]{:S(2)}) %copy-start.2) | copy-done | bytes 8216
  3.7 0.0 copy-start.3
  3.7 0.7 %copy-done.3 = s32[1,128,8]{1,2,0:T(8,128)S(1)} copy-done((s32[1,128,8]{1,2,0:T(8,128)S(1)}, s32[1,128,8]{1,2,0:T(8,128)}, u32[]{:S(2)}) %copy-start.3) | copy-done | bytes 4120
  4.4 0.0 copy-start.4
  4.4 0.7 %copy-done.4 = bf16[1,128,8]{1,2,0:T(8,128)(2,1)S(1)} copy-done((bf16[1,128,8]{1,2,0:T(8,128)(2,1)S(1)}, bf16[1,128,8]{1,2,0:T(8,128)(2,1)}, u32[]{:S(2)}) %copy-start.4) | copy-done | bytes 2072
  5.1 14.2 %shard_map.55 = (bf16[8,16,896]{2,1,0:T(8,128)(2,1)S(1)}, bf16[2,16,256]{2,1,0:T(8,128)(2,1)S(1)}) custom-call(s32[8,128]{1,0:T(8,128)S(1)} %bitcast.11, bf16[8,128]{1,0:T(8,128)(2,1)S(1)} %bitcast.12, bf16[128,7168]{1,0:T(8,128)(2,1)S(1)} %bitcast.9, bf16[128,7168]{1,0:T(8,128)(2,1)S(1)} %copy-done.1, bf16[16,256]{1,0:T(8,128)(2,1)S(1)} %bitcast.10), custom_call_target="tpu_custom_call" | custom-call | tf_op jit(solution)/shard_map/pallas_call | solution.py:249
  19.2 2.0 %shard_map.56 = bf16[3584,256]{1,0:T(8,128)(2,1)} custom-call(bf16[8,16,896]{2,1,0:T(8,128)(2,1)S(1)} %get-tuple-element.7.rows_ref, bf16[2,16,256]{2,1,0:T(8,128)(2,1)S(1)} %get-tuple-element.8.inputs_ref), custom_call_target="tpu_custom_call" | custom-call | tf_op jit(solution)/shard_map/pallas_call | solution.py:282
Async XLA Ops:
  0.0 1.5 %copy-start = (bf16[1,128,7168]{2,1,0:T(8,128)(2,1)S(1)}, bf16[1,128,7168]{2,1,0:T(8,128)(2,1)}, u32[]{:S(2)}) copy-start(bf16[1,128,7168]{2,1,0:T(8,128)(2,1)} %param.5) | copy-start | bytes 5505028
  1.5 1.5 %copy-start.1 = (bf16[128,7168]{1,0:T(8,128)(2,1)S(1)}, bf16[128,7168]{1,0:T(8,128)(2,1)}, u32[]{:S(2)}) copy-start(bf16[128,7168]{1,0:T(8,128)(2,1)} %loss_hbm.1) | copy-start | bytes 5505028
  3.0 0.7 %copy-start.2 = (bf16[1,1,16,256]{3,2,1,0:T(8,128)(2,1)S(1)}, bf16[1,1,16,256]{3,2,1,0:T(8,128)(2,1)}, u32[]{:S(2)}) copy-start(bf16[1,1,16,256]{3,2,1,0:T(8,128)(2,1)} %param.9) | copy-start | bytes 24580
  3.7 0.7 %copy-start.3 = (s32[1,128,8]{1,2,0:T(8,128)S(1)}, s32[1,128,8]{1,2,0:T(8,128)}, u32[]{:S(2)}) copy-start(s32[1,128,8]{1,2,0:T(8,128)} %param.7) | copy-start | bytes 12292
  4.4 0.7 %copy-start.4 = (bf16[1,128,8]{1,2,0:T(8,128)(2,1)S(1)}, bf16[1,128,8]{1,2,0:T(8,128)(2,1)}, u32[]{:S(2)}) copy-start(bf16[1,128,8]{1,2,0:T(8,128)(2,1)} %param.8) | copy-start | bytes 6148

commit v2 on v1

--- a/solution.py
+++ b/solution.py
@@ -12,7 +12,7 @@
 TILE = 16
 LANES = 128
 VMEM = pl.BlockSpec(memory_space=pltpu.VMEM)
-ANY = pl.BlockSpec(memory_space=pl.ANY)
+HBM = pl.BlockSpec(memory_space=pltpu.HBM)
 
 
 def each(count, body):
@@ -51,10 +51,10 @@
 
 
 def gather_kernel(
-    cap, ids_ref, gate_ref, grad_hbm, loss_hbm, inputs_ref,
+    cap, ids_hbm, gate_hbm, grad_hbm, loss_hbm, inputs_hbm,
     rows_ref, all_inputs_ref,
-    sel_own, sel_in, grad_v, loss_v, out_a, out_b,
-    load_sem, sel_sem, in_send, in_recv, send_a, send_b, recv_sem,
+    ids_ref, gate_ref, inputs_ref, sel_own, sel_in, grad_v, loss_v, out_a, out_b,
+    small_sem, load_sem, sel_sem, in_send, in_recv, send_a, send_b, recv_sem,
 ):
     pipes, cols, groups = lax.axis_size("pipe"), lax.axis_size("expert"), lax.axis_size("dp")
     p, e, g = lax.axis_index("pipe"), lax.axis_index("expert"), lax.axis_index("dp")
@@ -105,15 +105,12 @@
     def other_device(k):
         return lax.rem(me + 1 + k, count)
 
-    @pl.when(last)
-    def _():
-        for h in range(groups):
-            load(loss_hbm, loss_v, groups, h).start()
-
-    @pl.when(p >= 1)
-    def _():
-        for h in range(groups):
-            load(grad_hbm, grad_v, 0, h).start()
+    small = [
+        pltpu.make_async_copy(src, dst, small_sem.at[i])
+        for i, (src, dst) in enumerate(((ids_hbm, ids_ref), (gate_hbm, gate_ref), (inputs_hbm, inputs_ref)))
+    ]
+    for copy in small:
+        copy.start()
 
     barrier = pltpu.get_barrier_semaphore()
 
@@ -140,6 +137,18 @@
             greet(p, i // groups, i % groups)
         each(count - 1, one)
 
+    @pl.when(last)
+    def _():
+        for h in range(groups):
+            load(loss_hbm, loss_v, groups, h).start()
+
+    @pl.when(p >= 1)
+    def _():
+        for h in range(groups):
+            load(grad_hbm, grad_v, 0, h).start()
+
+    for copy in small:
+        copy.wait()
     ids = ids_ref[...]
     gates = gate_ref[...].astype(jnp.float32)
     for x in range(experts):
@@ -212,7 +221,7 @@
         ).wait()
 
 
-def product_kernel(cap, starts, rows_ref, inputs_ref, out_ref):
+def product_kernel(cap, starts, rows_ref, inputs_ref, out_hbm, out_ref, sem):
     sources, tile, size = rows_ref.shape
     pack = tile // cap
     depth = sources * tile
@@ -226,11 +235,26 @@
     weights = jnp.concatenate(
         [jnp.where(chunk == c, wide, 0.0).astype(jnp.bfloat16) for c in range(pack)], axis=1
     )
+    apart = all(starts[c] == c * size for c in range(pack))
+    copies = []
+
+    def flush(first, rows):
+        span = pl.ds(first, rows)
+        copies.append(pltpu.make_async_copy(out_ref.at[span], out_hbm.at[span], sem.at[len(copies)]))
+        copies[-1].start()
+
     for k in range(size // LANES):
         part = rows_ref[:, :, k * LANES:(k + 1) * LANES].reshape(depth, LANES)
         value = dot(part, weights, ((0,), (0,))).astype(out_ref.dtype)
         for c in range(pack):
-            out_ref[starts[c] + k * LANES:starts[c] + (k + 1) * LANES, :] = value[:, c * hidden:(c + 1) * hidden]
+            first = starts[c] + k * LANES
+            out_ref[first:first + LANES, :] = value[:, c * hidden:(c + 1) * hidden]
+            if apart:
+                flush(first, LANES)
+    if not apart:
+        flush(0, out_ref.shape[0])
+    for copy in copies:
+        copy.wait()
 
 
 def local(section_grad, loss_grad, expert_ids, gate_values, down_inputs):
@@ -252,15 +276,19 @@
             jax.ShapeDtypeStruct((count, TILE, size), bf16),
             jax.ShapeDtypeStruct((groups, slots, hidden), bf16),
         ],
-        in_specs=[VMEM, VMEM, ANY, ANY, VMEM],
+        in_specs=[HBM] * 5,
         out_specs=[VMEM, VMEM],
         scratch_shapes=[
+            pltpu.VMEM((topk, tokens), expert_ids.dtype),
+            pltpu.VMEM((topk, tokens), bf16),
+            pltpu.VMEM((slots, hidden), bf16),
             pltpu.VMEM((experts, TILE, tokens), bf16),
             pltpu.VMEM((experts, TILE, tokens), bf16),
             pltpu.VMEM((tokens, depth), bf16),
             pltpu.VMEM((tokens, depth), bf16),
             pltpu.VMEM((experts * groups, TILE, size), bf16),
             pltpu.VMEM((experts * groups, TILE, size), bf16),
+            dma((3,)),
             dma((2 * groups,)),
             dma((2,)),
             dma((groups,)),
@@ -283,7 +311,8 @@
         functools.partial(product_kernel, cap, starts),
         out_shape=jax.ShapeDtypeStruct((width, hidden), bf16),
         in_specs=[VMEM, VMEM],
-        out_specs=VMEM,
+        out_specs=HBM,
+        scratch_shapes=[pltpu.VMEM((width, hidden), bf16), dma((pack * (size // LANES),))],
         compiler_params=pltpu.CompilerParams(vmem_limit_bytes=32 << 20),
     )(rows, inputs)
     return out[None]

time: 21.5 us -> 21.2 us (0.986)
  the two profiles are of different devices: /device:TPU:6 before, /device:TPU:3 now
where the time goes in v2:
time: 21.2 us; the launch traced here: 20.9 us
  Pallas kernels  15.8 us (75%)
  local copies, waits for them, and re-layouts  5.06 us (24%)
    pallas_call x1, Pallas kernels, local(): pl.pallas_call(functools.partial(gather_kernel, cap), out_shape=[jax.Shap...  14 us
    unnamed x10, local copies, waits for them, and re-layouts  5.06 us
    pallas_call x1, Pallas kernels, local(): pl.pallas_call(functools.partial(product_kernel, cap, starts), out_shape=...  1.77 us

profile of v2, /device:TPU:3, one launch (start us, length us, event | category | flops | bytes accessed | tf_op | source)
XLA Modules:
  0.0 20.9 jit_solution(729189828173459457)
XLA Ops:
  0.0 0.0 copy-start
  0.0 1.5 %copy-done = bf16[1,128,7168]{2,1,0:T(8,128)(2,1)S(1)} copy-done((bf16[1,128,7168]{2,1,0:T(8,128)(2,1)S(1)}, bf16[1,128,7168]{2,1,0:T(8,128)(2,1)}, u32[]{:S(2)}) %copy-start) | copy-done | bytes 1835032
  1.5 0.0 copy-start.1
  1.5 1.5 %copy-done.1 = bf16[128,7168]{1,0:T(8,128)(2,1)S(1)} copy-done((bf16[128,7168]{1,0:T(8,128)(2,1)S(1)}, bf16[128,7168]{1,0:T(8,128)(2,1)}, u32[]{:S(2)}) %copy-start.1) | copy-done | bytes 1835032
  3.0 0.0 copy-start.2
  3.0 0.7 %copy-done.2 = bf16[1,1,16,256]{3,2,1,0:T(8,128)(2,1)S(1)} copy-done((bf16[1,1,16,256]{3,2,1,0:T(8,128)(2,1)S(1)}, bf16[1,1,16,256]{3,2,1,0:T(8,128)(2,1)}, u32[]{:S(2)}) %copy-start.2) | copy-done | bytes 8216
  3.7 0.0 copy-start.3
  3.7 0.7 %copy-done.3 = s32[1,128,8]{1,2,0:T(8,128)S(1)} copy-done((s32[1,128,8]{1,2,0:T(8,128)S(1)}, s32[1,128,8]{1,2,0:T(8,128)}, u32[]{:S(2)}) %copy-start.3) | copy-done | bytes 4120
  4.4 0.0 copy-start.4
  4.4 0.7 %copy-done.4 = bf16[1,128,8]{1,2,0:T(8,128)(2,1)S(1)} copy-done((bf16[1,128,8]{1,2,0:T(8,128)(2,1)S(1)}, bf16[1,128,8]{1,2,0:T(8,128)(2,1)}, u32[]{:S(2)}) %copy-start.4) | copy-done | bytes 2072
  5.1 14.0 %shard_map.55 = (bf16[8,16,896]{2,1,0:T(8,128)(2,1)S(1)}, bf16[2,16,256]{2,1,0:T(8,128)(2,1)S(1)}) custom-call(s32[8,128]{1,0:T(8,128)S(1)} %bitcast.11, bf16[8,128]{1,0:T(8,128)(2,1)S(1)} %bitcast.12, bf16[128,7168]{1,0:T(8,128)(2,1)S(1)} %bitcast.9, bf16[128,7168]{1,0:T(8,128)(2,1)S(1)} %copy-done.1, bf16[16,256]{1,0:T(8,128)(2,1)S(1)} %bitcast.10), custom_call_target="tpu_custom_call" | custom-call | tf_op jit(solution)/shard_map/pallas_call | solution.py:273
  19.1 1.8 %shard_map.56 = bf16[3584,256]{1,0:T(8,128)(2,1)} custom-call(bf16[8,16,896]{2,1,0:T(8,128)(2,1)S(1)} %get-tuple-element.7.rows_ref, bf16[2,16,256]{2,1,0:T(8,128)(2,1)S(1)} %get-tuple-element.8.inputs_ref), custom_call_target="tpu_custom_call" | custom-call | tf_op jit(solution)/shard_map/pallas_call | solution.py:310
Async XLA Ops:
  0.0 1.5 %copy-start = (bf16[1,128,7168]{2,1,0:T(8,128)(2,1)S(1)}, bf16[1,128,7168]{2,1,0:T(8,128)(2,1)}, u32[]{:S(2)}) copy-start(bf16[1,128,7168]{2,1,0:T(8,128)(2,1)} %param.5) | copy-start | bytes 5505028
  1.5 1.5 %copy-start.1 = (bf16[128,7168]{1,0:T(8,128)(2,1)S(1)}, bf16[128,7168]{1,0:T(8,128)(2,1)}, u32[]{:S(2)}) copy-start(bf16[128,7168]{1,0:T(8,128)(2,1)} %loss_hbm.1) | copy-start | bytes 5505028
  3.0 0.7 %copy-start.2 = (bf16[1,1,16,256]{3,2,1,0:T(8,128)(2,1)S(1)}, bf16[1,1,16,256]{3,2,1,0:T(8,128)(2,1)}, u32[]{:S(2)}) copy-start(bf16[1,1,16,256]{3,2,1,0:T(8,128)(2,1)} %param.9) | copy-start | bytes 24580
  3.7 0.7 %copy-start.3 = (s32[1,128,8]{1,2,0:T(8,128)S(1)}, s32[1,128,8]{1,2,0:T(8,128)}, u32[]{:S(2)}) copy-start(s32[1,128,8]{1,2,0:T(8,128)} %param.7) | copy-start | bytes 12292
  4.4 0.7 %copy-start.4 = (bf16[1,128,8]{1,2,0:T(8,128)(2,1)S(1)}, bf16[1,128,8]{1,2,0:T(8,128)(2,1)}, u32[]{:S(2)}) copy-start(bf16[1,128,8]{1,2,0:T(8,128)(2,1)} %param.8) | copy-start | bytes 6148

commit v3 on v2

--- a/solution.py
+++ b/solution.py
@@ -301,11 +301,16 @@
             collective_id=0, has_side_effects=True, vmem_limit_bytes=32 << 20
         ),
     )(
-        jnp.swapaxes(expert_ids[0], 0, 1),
-        jnp.swapaxes(gate_values[0], 0, 1),
-        section_grad[0],
-        loss_grad,
-        down_inputs[0, 0],
+        *(
+            pltpu.with_memory_space_constraint(x, pltpu.HBM)
+            for x in (
+                jnp.swapaxes(expert_ids[0], 0, 1),
+                jnp.swapaxes(gate_values[0], 0, 1),
+                section_grad[0],
+                loss_grad,
+                down_inputs[0, 0],
+            )
+        )
     )
     out = pl.pallas_call(
         functools.partial(product_kernel, cap, starts),

time: 21.2 us -> 16 us (0.75)
  local copies, waits for them, and re-layouts: 5.06 us -> 0 us
    unnamed x10 -> x0, local copies, waits for them, and re-layouts: 5.06 us -> none
where the time goes in v3:
time: 16 us; the launch traced here: 15.8 us
  Pallas kernels  15.8 us (99%)
    pallas_call x1, Pallas kernels, local(): pl.pallas_call(functools.partial(gather_kernel, cap), out_shape=[jax.Shap...  14 us
    pallas_call x1, Pallas kernels, local(): pl.pallas_call(functools.partial(product_kernel, cap, starts), out_shape=...  1.79 us

profile of v3, /device:TPU:3, one launch (start us, length us, event | category | flops | bytes accessed | tf_op | source)
XLA Modules:
  0.0 15.8 jit_solution(17048908383995247959)
XLA Ops:
  0.0 14.0 %shard_map.55 = (bf16[8,16,896]{2,1,0:T(8,128)(2,1)S(1)}, bf16[2,16,256]{2,1,0:T(8,128)(2,1)S(1)}) custom-call(s32[8,128]{1,0:T(8,128)} %bitcast.11, bf16[8,128]{1,0:T(8,128)(2,1)} %bitcast.12, bf16[128,7168]{1,0:T(8,128)(2,1)} %bitcast.9, bf16[128,7168]{1,0:T(8,128)(2,1)} %loss_hbm.1, bf16[16,256]{1,0:T(8,128)(2,1)} %bitcast.10), custom_call_target="tpu_custom_call" | custom-call | tf_op jit(solution)/shard_map/pallas_call | solution.py:273
  14.0 1.8 %shard_map.56 = bf16[3584,256]{1,0:T(8,128)(2,1)} custom-call(bf16[8,16,896]{2,1,0:T(8,128)(2,1)S(1)} %get-tuple-element.7.rows_ref, bf16[2,16,256]{2,1,0:T(8,128)(2,1)S(1)} %get-tuple-element.8.inputs_ref), custom_call_target="tpu_custom_call" | custom-call | tf_op jit(solution)/shard_map/pallas_call | solution.py:315

commit v4 on v3

--- a/solution.py
+++ b/solution.py
@@ -53,8 +53,8 @@
 def gather_kernel(
     cap, ids_hbm, gate_hbm, grad_hbm, loss_hbm, inputs_hbm,
     rows_ref, all_inputs_ref,
-    ids_ref, gate_ref, inputs_ref, sel_own, sel_in, grad_v, loss_v, out_a, out_b,
-    small_sem, load_sem, sel_sem, in_send, in_recv, send_a, send_b, recv_sem,
+    ids_ref, gate_ref, inputs_ref, sel_own, sel_in, grad_v, out,
+    small_sem, load_sem, sel_sem, in_send, in_recv, send_sem, recv_sem,
 ):
     pipes, cols, groups = lax.axis_size("pipe"), lax.axis_size("expert"), lax.axis_size("dp")
     p, e, g = lax.axis_index("pipe"), lax.axis_index("expert"), lax.axis_index("dp")
@@ -65,31 +65,31 @@
     size, starts = chunk_starts(width, pack)
     count = cols * groups
     me = e * groups + g
-    last = p == pipes - 1
+    after, before = lax.rem(p + 1, pipes), lax.rem(p + pipes - 1, pipes)
     slot = g * cols + e
 
     def place(pipe, col, group):
         return {"pipe": pipe, "expert": col, "dp": group}
 
-    def load(src, dst, base, h):
+    def load(src, h):
         span = pl.ds(h * width, width)
-        return pltpu.make_async_copy(src.at[:, span], dst.at[:, span], load_sem.at[base + h])
-
-    def row_copy(pipe, i, source, sems):
+        return pltpu.make_async_copy(src.at[:, span], grad_v.at[:, span], load_sem.at[h])
+
+    def row_copy(i):
         col, group = i // groups, i % groups
         return pltpu.make_async_remote_copy(
-            src_ref=source.at[(col // SPLIT) * groups + group],
+            src_ref=out.at[(col // SPLIT) * groups + group],
             dst_ref=rows_ref.at[slot],
-            send_sem=sems.at[i],
+            send_sem=send_sem.at[i],
             recv_sem=recv_sem.at[slot],
-            device_id=place(pipe, col, group),
+            device_id=place(before, col, group),
             device_id_type=pl.DeviceIdType.MESH,
         )
 
     def selector_copy():
         return pltpu.make_async_remote_copy(
             src_ref=sel_own, dst_ref=sel_in, send_sem=sel_sem.at[0], recv_sem=sel_sem.at[1],
-            device_id=place(lax.rem(p + 1, pipes), e, g), device_id_type=pl.DeviceIdType.MESH,
+            device_id=place(after, e, g), device_id_type=pl.DeviceIdType.MESH,
         )
 
     def inputs_copy(group):
@@ -101,9 +101,6 @@
 
     def other_group(k):
         return lax.rem(g + 1 + k, groups)
-
-    def other_device(k):
-        return lax.rem(me + 1 + k, count)
 
     small = [
         pltpu.make_async_copy(src, dst, small_sem.at[i])
@@ -119,33 +116,20 @@
             barrier, inc=1, device_id=place(pipe, col, group), device_id_type=pl.DeviceIdType.MESH
         )
 
-    @pl.when(p >= 1)
-    def _():
-        greet(p - 1, e, g)
-
+    greet(before, e, g)
     for k in range(groups - 1):
         greet(p, e, other_group(k))
-
-    @pl.when(jnp.logical_not(last))
-    def _():
-        each(count, lambda i: greet(p + 1, i // groups, i % groups))
-
-    @pl.when(last)
-    def _():
-        def one(k):
-            i = other_device(k)
-            greet(p, i // groups, i % groups)
-        each(count - 1, one)
-
-    @pl.when(last)
+    each(count, lambda i: greet(after, i // groups, i % groups))
+
+    @pl.when(p == 0)
     def _():
         for h in range(groups):
-            load(loss_hbm, loss_v, groups, h).start()
+            load(loss_hbm, h).start()
 
     @pl.when(p >= 1)
     def _():
         for h in range(groups):
-            load(grad_hbm, grad_v, 0, h).start()
+            load(grad_hbm, h).start()
 
     for copy in small:
         copy.wait()
@@ -155,63 +139,37 @@
         sel_own[x] = make_selector(ids, gates, x, cap)
     all_inputs_ref[g] = inputs_ref[...]
 
-    targets = groups - 1 + jnp.where(p >= 1, count, 0) + jnp.where(last, count - 1, 1)
-    pl.semaphore_wait(barrier, targets)
-
-    @pl.when(jnp.logical_not(last))
-    def _():
-        selector_copy().start()
-
+    pl.semaphore_wait(barrier, count + groups)
+    selector_copy().start()
     for k in range(groups - 1):
         inputs_copy(other_group(k)).start()
 
-    def pick(sel_ref, values, out, h):
+    def pick(h):
         for x in range(experts):
-            sel = sel_ref[x].astype(jnp.float32)
+            sel = sel_in[x].astype(jnp.float32)
             chunk = lax.broadcasted_iota(jnp.int32, sel.shape, 0) // cap
             total = None
             for c in range(pack):
                 part = jnp.where(chunk == c, sel, 0.0).astype(jnp.bfloat16)
-                term = dot(part, values[:, pl.ds(h * width + starts[c], size)], ((1,), (0,)))
+                term = dot(part, grad_v[:, pl.ds(h * width + starts[c], size)], ((1,), (0,)))
                 total = term if total is None else total + term
             out[x * groups + h] = total.astype(jnp.bfloat16)
 
-    @pl.when(last)
-    def _():
-        for h in range(groups):
-            load(loss_hbm, loss_v, groups, h).wait()
-            pick(sel_own, loss_v, out_b, h)
-        rows_ref[slot] = out_b[(e // SPLIT) * groups + g]
-        each(count - 1, lambda k: row_copy(p, other_device(k), out_b, send_b).start())
-
-    @pl.when(p >= 1)
-    def _():
-        selector_copy().wait_recv()
-        for h in range(groups):
-            load(grad_hbm, grad_v, 0, h).wait()
-            pick(sel_in, grad_v, out_a, h)
-            each(cols, lambda k: row_copy(p - 1, k * groups + h, out_a, send_a).start())
+    selector_copy().wait_recv()
+    for h in range(groups):
+        load(grad_hbm, h).wait()
+        pick(h)
+        each(cols, lambda k: row_copy(lax.rem(e + 1 + k, cols) * groups + h).start())
 
     def arrived(i):
         return pltpu.make_async_remote_copy(
-            src_ref=out_a.at[0], dst_ref=rows_ref.at[i], send_sem=send_a.at[0], recv_sem=recv_sem.at[i],
+            src_ref=out.at[0], dst_ref=rows_ref.at[i], send_sem=send_sem.at[0], recv_sem=recv_sem.at[i],
             device_id=place(p, e, g), device_id_type=pl.DeviceIdType.MESH,
         )
 
-    @pl.when(jnp.logical_not(last))
-    def _():
-        each(count, lambda i: arrived(i).wait_recv())
-        selector_copy().wait_send()
-
-    @pl.when(last)
-    def _():
-        each(count - 1, lambda k: arrived(lax.rem(slot + 1 + k, count)).wait_recv())
-        each(count - 1, lambda k: row_copy(p, other_device(k), out_b, send_b).wait_send())
-
-    @pl.when(p >= 1)
-    def _():
-        each(count, lambda i: row_copy(p - 1, i, out_a, send_a).wait_send())
-
+    each(count, lambda i: arrived(i).wait_recv())
+    selector_copy().wait_send()
+    each(count, lambda i: row_copy(i).wait_send())
     for k in range(groups - 1):
         group = other_group(k)
         pltpu.make_async_remote_copy(
@@ -285,15 +243,12 @@
             pltpu.VMEM((experts, TILE, tokens), bf16),
             pltpu.VMEM((experts, TILE, tokens), bf16),
             pltpu.VMEM((tokens, depth), bf16),
-            pltpu.VMEM((tokens, depth), bf16),
-            pltpu.VMEM((experts * groups, TILE, size), bf16),
             pltpu.VMEM((experts * groups, TILE, size), bf16),
             dma((3,)),
-            dma((2 * groups,)),
+            dma((groups,)),
             dma((2,)),
             dma((groups,)),
             dma((groups,)),
-            dma((count,)),
             dma((count,)),
             dma((count,)),
         ],

time: 16 us -> 14.9 us (0.931)
  the two profiles are of different devices: /device:TPU:3 before, /device:TPU:1 now
where the time goes in v4:
time: 14.9 us; the launch traced here: 14.7 us
  Pallas kernels  14.7 us (99%)
    pallas_call x1, Pallas kernels, local(): pl.pallas_call(functools.partial(gather_kernel, cap), out_shape=[jax.Shap...  12.9 us
    pallas_call x1, Pallas kernels, local(): pl.pallas_call(functools.partial(product_kernel, cap, starts), out_shape=...  1.78 us

profile of v4, /device:TPU:1, one launch (start us, length us, event | category | flops | bytes accessed | tf_op | source)
XLA Modules:
  0.0 14.7 jit_solution(16497797489925119030)
XLA Ops:
  0.0 12.9 %shard_map.55 = (bf16[8,16,896]{2,1,0:T(8,128)(2,1)S(1)}, bf16[2,16,256]{2,1,0:T(8,128)(2,1)S(1)}) custom-call(s32[8,128]{1,0:T(8,128)} %bitcast.11, bf16[8,128]{1,0:T(8,128)(2,1)} %bitcast.12, bf16[128,7168]{1,0:T(8,128)(2,1)} %bitcast.9, bf16[128,7168]{1,0:T(8,128)(2,1)} %loss_hbm.1, bf16[16,256]{1,0:T(8,128)(2,1)} %bitcast.10), custom_call_target="tpu_custom_call" | custom-call | tf_op jit(solution)/shard_map/pallas_call | solution.py:231
  12.9 1.8 %shard_map.56 = bf16[3584,256]{1,0:T(8,128)(2,1)} custom-call(bf16[8,16,896]{2,1,0:T(8,128)(2,1)S(1)} %get-tuple-element.7.rows_ref, bf16[2,16,256]{2,1,0:T(8,128)(2,1)S(1)} %get-tuple-element.8.inputs_ref), custom_call_target="tpu_custom_call" | custom-call | tf_op jit(solution)/shard_map/pallas_call | solution.py:270

commit v5 on v4

--- a/solution.py
+++ b/solution.py
@@ -52,8 +52,8 @@
 
 def gather_kernel(
     cap, ids_hbm, gate_hbm, grad_hbm, loss_hbm, inputs_hbm,
-    rows_ref, all_inputs_ref,
-    ids_ref, gate_ref, inputs_ref, sel_own, sel_in, grad_v, out,
+    rows_ref, weights_ref,
+    all_inputs_ref, ids_ref, gate_ref, inputs_ref, sel_own, sel_in, grad_v, out,
     small_sem, load_sem, sel_sem, in_send, in_recv, send_sem, recv_sem,
 ):
     pipes, cols, groups = lax.axis_size("pipe"), lax.axis_size("expert"), lax.axis_size("dp")
@@ -161,15 +161,6 @@
         pick(h)
         each(cols, lambda k: row_copy(lax.rem(e + 1 + k, cols) * groups + h).start())
 
-    def arrived(i):
-        return pltpu.make_async_remote_copy(
-            src_ref=out.at[0], dst_ref=rows_ref.at[i], send_sem=send_sem.at[0], recv_sem=recv_sem.at[i],
-            device_id=place(p, e, g), device_id_type=pl.DeviceIdType.MESH,
-        )
-
-    each(count, lambda i: arrived(i).wait_recv())
-    selector_copy().wait_send()
-    each(count, lambda i: row_copy(i).wait_send())
     for k in range(groups - 1):
         group = other_group(k)
         pltpu.make_async_remote_copy(
@@ -177,22 +168,38 @@
             send_sem=in_send.at[group], recv_sem=in_recv.at[group],
             device_id=place(p, e, group), device_id_type=pl.DeviceIdType.MESH,
         ).wait()
-
-
-def product_kernel(cap, starts, rows_ref, inputs_ref, out_hbm, out_ref, sem):
-    sources, tile, size = rows_ref.shape
-    pack = tile // cap
-    depth = sources * tile
-    groups, slots, hidden = inputs_ref.shape
-    inputs = inputs_ref[...].reshape(groups * slots, hidden)
+    weights_ref[...] = spread_inputs(all_inputs_ref[...], cap, count * TILE)
+
+    def arrived(i):
+        return pltpu.make_async_remote_copy(
+            src_ref=out.at[0], dst_ref=rows_ref.at[i], send_sem=send_sem.at[0], recv_sem=recv_sem.at[i],
+            device_id=place(p, e, g), device_id_type=pl.DeviceIdType.MESH,
+        )
+
+    each(count, lambda i: arrived(i).wait_recv())
+    selector_copy().wait_send()
+    each(count, lambda i: row_copy(i).wait_send())
+
+
+def spread_inputs(inputs, cap, depth):
+    groups, slots, hidden = inputs.shape
+    inputs = inputs.reshape(groups * slots, hidden)
     r = lax.broadcasted_iota(jnp.int32, (depth, groups * slots), 0)
     s = lax.broadcasted_iota(jnp.int32, (depth, groups * slots), 1)
-    spread = jnp.where((r // tile == s // cap) & (r % cap == s % cap), 1.0, 0.0).astype(jnp.bfloat16)
+    spread = jnp.where((r // TILE == s // cap) & (r % cap == s % cap), 1.0, 0.0).astype(jnp.bfloat16)
     wide = dot(spread, inputs, ((1,), (0,)))
-    chunk = (lax.broadcasted_iota(jnp.int32, wide.shape, 0) // cap) % pack
-    weights = jnp.concatenate(
-        [jnp.where(chunk == c, wide, 0.0).astype(jnp.bfloat16) for c in range(pack)], axis=1
-    )
+    chunk = (lax.broadcasted_iota(jnp.int32, wide.shape, 0) // cap) % (TILE // cap)
+    return jnp.concatenate(
+        [jnp.where(chunk == c, wide, 0.0).astype(jnp.bfloat16) for c in range(TILE // cap)], axis=1
+    )
+
+
+def product_kernel(starts, rows_ref, weights_ref, out_hbm, out_ref, sem):
+    sources, tile, size = rows_ref.shape
+    pack = len(starts)
+    depth = sources * tile
+    hidden = out_ref.shape[1]
+    weights = weights_ref[...]
     apart = all(starts[c] == c * size for c in range(pack))
     copies = []
 
@@ -228,15 +235,16 @@
     count = cols * groups
     bf16 = jnp.bfloat16
     dma = pltpu.SemaphoreType.DMA
-    rows, inputs = pl.pallas_call(
+    rows, weights = pl.pallas_call(
         functools.partial(gather_kernel, cap),
         out_shape=[
             jax.ShapeDtypeStruct((count, TILE, size), bf16),
-            jax.ShapeDtypeStruct((groups, slots, hidden), bf16),
+            jax.ShapeDtypeStruct((count * TILE, pack * hidden), bf16),
         ],
         in_specs=[HBM] * 5,
         out_specs=[VMEM, VMEM],
         scratch_shapes=[
+            pltpu.VMEM((groups, slots, hidden), bf16),
             pltpu.VMEM((topk, tokens), expert_ids.dtype),
             pltpu.VMEM((topk, tokens), bf16),
             pltpu.VMEM((slots, hidden), bf16),
@@ -268,13 +276,13 @@
         )
     )
     out = pl.pallas_call(
-        functools.partial(product_kernel, cap, starts),
+        functools.partial(product_kernel, starts),
         out_shape=jax.ShapeDtypeStruct((width, hidden), bf16),
         in_specs=[VMEM, VMEM],
         out_specs=HBM,
         scratch_shapes=[pltpu.VMEM((width, hidden), bf16), dma((pack * (size // LANES),))],
         compiler_params=pltpu.CompilerParams(vmem_limit_bytes=32 << 20),
-    )(rows, inputs)
+    )(rows, weights)
     return out[None]
 
 

time: 14.9 us -> 14.7 us (0.987)
  no operation moved by 1% of the time
where the time goes in v5:
time: 14.7 us; the launch traced here: 14.6 us
  Pallas kernels  14.6 us (99%)
    pallas_call x1, Pallas kernels, local(): pl.pallas_call(functools.partial(gather_kernel, cap), out_shape=[jax.Shap...  12.9 us
    pallas_call x1, Pallas kernels, local(): pl.pallas_call(functools.partial(product_kernel, starts), out_shape=jax.S...  1.67 us

profile of v5, /device:TPU:1, one launch (start us, length us, event | category | flops | bytes accessed | tf_op | source)
XLA Modules:
  0.0 14.6 jit_solution(9516087606534527025)
XLA Ops:
  0.0 12.9 %shard_map.55 = (bf16[8,16,896]{2,1,0:T(8,128)(2,1)S(1)}, bf16[128,1024]{1,0:T(8,128)(2,1)S(1)}) custom-call(s32[8,128]{1,0:T(8,128)} %bitcast.11, bf16[8,128]{1,0:T(8,128)(2,1)} %bitcast.12, bf16[128,7168]{1,0:T(8,128)(2,1)} %bitcast.9, bf16[128,7168]{1,0:T(8,128)(2,1)} %loss_hbm.1, bf16[16,256]{1,0:T(8,128)(2,1)} %bitcast.10), custom_call_target="tpu_custom_call" | custom-call | tf_op jit(solution)/shard_map/pallas_call | solution.py:238
  12.9 1.7 %shard_map.56 = bf16[3584,256]{1,0:T(8,128)(2,1)} custom-call(bf16[8,16,896]{2,1,0:T(8,128)(2,1)S(1)} %get-tuple-element.7.rows_ref, bf16[128,1024]{1,0:T(8,128)(2,1)S(1)} %get-tuple-element.8.weights_ref), custom_call_target="tpu_custom_call" | custom-call | tf_op jit(solution)/shard_map/pallas_call | solution.py:278

commit v6 on v5

--- a/solution.py
+++ b/solution.py
@@ -32,18 +32,19 @@
     return size, [min(c * size, width - size) for c in range(pack)]
 
 
-def make_selector(ids, gates, expert, cap):
+def earlier_tokens(tokens):
+    shape = (tokens, tokens)
+    earlier = lax.broadcasted_iota(jnp.int32, shape, 0) < lax.broadcasted_iota(jnp.int32, shape, 1)
+    return jnp.where(earlier, 1.0, 0.0).astype(jnp.bfloat16)
+
+
+def make_selector(ids, gates, before, expert, cap):
     tokens = ids.shape[1]
     found = ids == expert
-    ones = jnp.ones((TILE, ids.shape[0]), jnp.float32)
     hit = jnp.sum(jnp.where(found, 1.0, 0.0), axis=0, keepdims=True)
     gate = jnp.sum(jnp.where(found, gates, 0.0), axis=0, keepdims=True)
     hit = jnp.broadcast_to(hit, (TILE, tokens))
     gate = jnp.broadcast_to(gate, (TILE, tokens))
-    earlier = lax.broadcasted_iota(jnp.int32, (tokens, tokens), 0) < lax.broadcasted_iota(
-        jnp.int32, (tokens, tokens), 1
-    )
-    before = jnp.where(earlier, 1.0, 0.0).astype(jnp.bfloat16)
     rank = dot(hit.astype(jnp.bfloat16), before, ((1,), (0,)))
     row = lax.broadcasted_iota(jnp.int32, (TILE, tokens), 0) % cap
     keep = (hit > 0.5) & (rank.astype(jnp.int32) == row)
@@ -131,12 +132,13 @@
         for h in range(groups):
             load(grad_hbm, h).start()
 
+    earlier = earlier_tokens(ids_ref.shape[1])
     for copy in small:
         copy.wait()
     ids = ids_ref[...]
     gates = gate_ref[...].astype(jnp.float32)
     for x in range(experts):
-        sel_own[x] = make_selector(ids, gates, x, cap)
+        sel_own[x] = make_selector(ids, gates, earlier, x, cap)
     all_inputs_ref[g] = inputs_ref[...]
 
     pl.semaphore_wait(barrier, count + groups)
@@ -149,9 +151,11 @@
             sel = sel_in[x].astype(jnp.float32)
             chunk = lax.broadcasted_iota(jnp.int32, sel.shape, 0) // cap
             total = None
-            for c in range(pack):
-                part = jnp.where(chunk == c, sel, 0.0).astype(jnp.bfloat16)
-                term = dot(part, grad_v[:, pl.ds(h * width + starts[c], size)], ((1,), (0,)))
+            for c in range(0, pack, 2):
+                pair = range(c, min(c + 2, pack))
+                parts = [jnp.where(chunk == d, sel, 0.0).astype(jnp.bfloat16) for d in pair]
+                values = [grad_v[:, pl.ds(h * width + starts[d], size)] for d in pair]
+                term = dot(jnp.concatenate(parts, axis=1), jnp.concatenate(values, axis=0), ((1,), (0,)))
                 total = term if total is None else total + term
             out[x * groups + h] = total.astype(jnp.bfloat16)
 

time: 14.7 us -> 14.7 us (level)
  no operation moved by 1% of the time
where the time goes in v6:
time: 14.7 us; the launch traced here: 14.6 us
  Pallas kernels  14.6 us (99%)
    pallas_call x1, Pallas kernels, local(): pl.pallas_call(functools.partial(gather_kernel, cap), out_shape=[jax.Shap...  12.9 us
    pallas_call x1, Pallas kernels, local(): pl.pallas_call(functools.partial(product_kernel, starts), out_shape=jax.S...  1.67 us

profile of v6, /device:TPU:1, one launch (start us, length us, event | category | flops | bytes accessed | tf_op | source)
XLA Modules:
  0.0 14.6 jit_solution(15806040055833160201)
XLA Ops:
  0.0 12.9 %shard_map.55 = (bf16[8,16,896]{2,1,0:T(8,128)(2,1)S(1)}, bf16[128,1024]{1,0:T(8,128)(2,1)S(1)}) custom-call(s32[8,128]{1,0:T(8,128)} %bitcast.11, bf16[8,128]{1,0:T(8,128)(2,1)} %bitcast.12, bf16[128,7168]{1,0:T(8,128)(2,1)} %bitcast.9, bf16[128,7168]{1,0:T(8,128)(2,1)} %loss_hbm.1, bf16[16,256]{1,0:T(8,128)(2,1)} %bitcast.10), custom_call_target="tpu_custom_call" | custom-call | tf_op jit(solution)/shard_map/pallas_call | solution.py:242
  12.9 1.7 %shard_map.56 = bf16[3584,256]{1,0:T(8,128)(2,1)} custom-call(bf16[8,16,896]{2,1,0:T(8,128)(2,1)S(1)} %get-tuple-element.7.rows_ref, bf16[128,1024]{1,0:T(8,128)(2,1)S(1)} %get-tuple-element.8.weights_ref), custom_call_target="tpu_custom_call" | custom-call | tf_op jit(solution)/shard_map/pallas_call | solution.py:282
